TPU v7x, 512 devices: a whole 4x8x8 slice. The times are simulated.
512 devices in a mesh: section: 8 (over x, core), peer: 64 (over y, z).
Axes of the slice: x: 4, y: 8, z: 8, core: 2. Of those that a mesh axis runs over, the one named last changes fastest.
Arguments:
- rows_in: bfloat16 [8, 8192, 5120], P('section', 'peer')
- returned: bfloat16 [8, 8192, 5120], P('section', 'peer'), may hold values from -6 to 6
- norm_gain: bfloat16 [8, 5120], P('section'), may hold values from 0.099609375 to 1.8984375
- adapter_down: bfloat16 [8, 5120, 16], P('section'), may hold values from -0.078125 to 0.078125
- adapter_up: bfloat16 [8, 16, 5120], P('section'), may hold values from -1.5 to 1.5
- wiring: int32 [8, 64], P('section', 'peer'), may hold values from 0 to 63, as said below
Outputs:
- forward_rows: bfloat16 [8, 8192, 5120], P('section', 'peer')
- grad_down: float32 [8, 5120, 16], P('section')
- grad_up: float32 [8, 16, 5120], P('section')
Inputs may be any that keep to these rules, and one draw needn't show every extreme that they name: For each section s there is a mask m below 16 with wiring[s, p] = p XOR m for every peer p; each section's entries are a permutation of the peers.
All inputs are finite; a program needn't handle non-finite values.
Results may differ from a plain program's by a relative error of at most 0.0058.
Values may be sent and summed in bfloat16 or wider, within the bound.
A program may use at most 64 MiB of HBM per device.

v0:
```python
import jax
import jax.numpy as jnp
from jax import lax
from jax.sharding import PartitionSpec as P

BITS = 4


EPSILON = 1e-05


def from_partner(value, axis, bit):
    mask = 2**bit
    pairs = [(source, source ^ mask) for source in range(lax.axis_size(axis))]
    return lax.ppermute(value, axis, pairs)


def passed_along(value, axis, by):
    count = lax.axis_size(axis)
    return lax.ppermute(value, axis, [(i, (i + by) % count) for i in range(count)])


def pick_moved(partner_bits, bit_index, moved, kept):
    flag = jnp.bitwise_and(jnp.right_shift(partner_bits, bit_index), 1) == 1
    return jnp.where(flag, moved, kept)


def contract_rows(left, right):
    return lax.dot_general(
        left, right, (((0,), (0,)), ((), ())), preferred_element_type=jnp.float32
    )


def times_transpose(left, right):
    return lax.dot_general(
        left, right, (((1,), (1,)), ((), ())), preferred_element_type=jnp.float32
    )


def shards(rows_in, returned, norm_gain, adapter_down, adapter_up, wiring):
    inputs_f = rows_in[0].astype(jnp.float32)
    mean_square = jnp.mean(inputs_f * inputs_f, axis=-1, keepdims=True)
    normed = (
        inputs_f * lax.rsqrt(mean_square + EPSILON) * norm_gain[0].astype(jnp.float32)
    ).astype(jnp.bfloat16)
    down_matrix = adapter_down[0]
    up_matrix = adapter_up[0]
    latent = jnp.dot(normed, down_matrix, preferred_element_type=jnp.float32).astype(jnp.bfloat16)
    outputs = (inputs_f + jnp.dot(latent, up_matrix, preferred_element_type=jnp.float32)).astype(
        jnp.bfloat16
    )
    partner_bits = jnp.bitwise_xor(wiring[0, 0], lax.axis_index("peer"))
    peer_count = lax.axis_size("peer")
    onward = outputs
    for bit_index in range(BITS):
        moved = from_partner(onward, "peer", bit_index)
        onward = pick_moved(partner_bits, bit_index, moved, onward)
    onward = passed_along(onward, "section", 1)
    upstream = passed_along(returned[0], "section", -1)
    for bit_index in range(BITS):
        moved = from_partner(upstream, "peer", bit_index)
        upstream = pick_moved(partner_bits, bit_index, moved, upstream)
    term_up = contract_rows(latent, upstream)
    latent_grad = times_transpose(upstream, up_matrix).astype(jnp.bfloat16)
    term_down = contract_rows(normed, latent_grad)
    sum_down, sum_up = lax.psum((term_down, term_up), "peer")
    return (onward[None], (sum_down / peer_count)[None], (sum_up / peer_count)[None])


def solution(mesh):
    in_specs = (
        P("section", "peer", None),
        P("section", "peer", None),
        P("section", None),
        P("section", None, None),
        P("section", None, None),
        P("section", "peer"),
    )
    out_specs = (P("section", "peer", None), P("section", None, None), P("section", None, None))
    return jax.shard_map(shards, mesh=mesh, in_specs=in_specs, out_specs=out_specs, check_vma=False)
```

profile of v0, /device:TPU:1, one launch (start us, length us, event | category | flops | bytes accessed | tf_op | source)
XLA Modules:
  0.0 564.7 jit_solution(2735380345768379773)
XLA Ops:
  7.2 6.9 %collective-permute-start.5 = (bf16[128,5120]{1,0:T(8,128)(2,1)}, bf16[128,5120]{1,0:T(8,128)(2,1)}, u32[]{:S(2)}, u32[]{:S(2)}) collective-permute-start(bf16[128,5120]{1,0:T(8,128)(2,1)} %bitcast.42), channel_id=1, source_target_pairs={{0,448},{64,0},{128,64},{192,128},{256,192},{320,256},{384,320},{4... | collective-permute-start | bytes 3932168 | tf_op jit(solution)/shard_map/ppermute | solution.py:20
  14.9 1.7 fusion.3
  16.6 1.4 fusion.17
  18.5 1.9 collective-permute-start
  20.5 5.3 collective-permute-done.5
  25.8 4.0 collective-permute-start.6
  30.4 20.4 %collective-permute-done = bf16[128,5120]{1,0:T(8,128)(2,1)} collective-permute-done((bf16[128,5120]{1,0:T(8,128)(2,1)S(1)}, bf16[128,5120]{1,0:T(8,128)(2,1)}, u32[]{:S(2)}, u32[]{:S(2)}) %collective-permute-start) | collective-permute-done | bytes 1310752 | tf_op jit(solution)/shard_map/ppermute | solution.py:15
  50.8 1.2 broadcast_select_fusion.1
  52.0 1.9 collective-permute-start.1
  53.9 45.6 %collective-permute-done.6 = bf16[128,5120]{1,0:T(8,128)(2,1)} collective-permute-done((bf16[128,5120]{1,0:T(8,128)(2,1)}, bf16[128,5120]{1,0:T(8,128)(2,1)}, u32[]{:S(2)}, u32[]{:S(2)}) %collective-permute-start.6) | collective-permute-done | bytes 1310752 | tf_op jit(solution)/shard_map/ppermute | solution.py:15
  99.4 2.5 broadcast_select_fusion
  101.9 1.9 collective-permute-start.7
  103.9 147.3 %collective-permute-done.1 = bf16[128,5120]{1,0:T(8,128)(2,1)} collective-permute-done((bf16[128,5120]{1,0:T(8,128)(2,1)}, bf16[128,5120]{1,0:T(8,128)(2,1)}, u32[]{:S(2)}, u32[]{:S(2)}) %collective-permute-start.1) | collective-permute-done | bytes 1310752 | tf_op jit(solution)/shard_map/ppermute | solution.py:15
  251.1 1.5 broadcast_select_fusion.3
  252.6 1.9 collective-permute-start.2
  254.5 24.8 %collective-permute-done.7 = bf16[128,5120]{1,0:T(8,128)(2,1)} collective-permute-done((bf16[128,5120]{1,0:T(8,128)(2,1)}, bf16[128,5120]{1,0:T(8,128)(2,1)}, u32[]{:S(2)}, u32[]{:S(2)}) %collective-permute-start.7) | collective-permute-done | bytes 1310752 | tf_op jit(solution)/shard_map/ppermute | solution.py:15
  279.3 2.5 broadcast_select_fusion.2
  281.8 4.2 collective-permute-start.8
  286.0 39.8 %collective-permute-done.2 = bf16[128,5120]{1,0:T(8,128)(2,1)} collective-permute-done((bf16[128,5120]{1,0:T(8,128)(2,1)S(1)}, bf16[128,5120]{1,0:T(8,128)(2,1)}, u32[]{:S(2)}, u32[]{:S(2)}) %collective-permute-start.2) | collective-permute-done | bytes 1310752 | tf_op jit(solution)/shard_map/ppermute | solution.py:15
  325.8 1.2 broadcast_select_fusion.5
  327.0 1.9 collective-permute-start.3
  328.9 37.8 %collective-permute-done.8 = bf16[128,5120]{1,0:T(8,128)(2,1)} collective-permute-done((bf16[128,5120]{1,0:T(8,128)(2,1)}, bf16[128,5120]{1,0:T(8,128)(2,1)}, u32[]{:S(2)}, u32[]{:S(2)}) %collective-permute-start.8) | collective-permute-done | bytes 1310752 | tf_op jit(solution)/shard_map/ppermute | solution.py:15
  366.7 1.5 broadcast_select_fusion.4
  368.2 1.9 collective-permute-start.9
  370.1 2.5 broadcast_select_fusion.7
  372.7 23.5 %collective-permute-done.9 = bf16[128,5120]{1,0:T(8,128)(2,1)} collective-permute-done((bf16[128,5120]{1,0:T(8,128)(2,1)S(1)}, bf16[128,5120]{1,0:T(8,128)(2,1)}, u32[]{:S(2)}, u32[]{:S(2)}) %collective-permute-start.9) | collective-permute-done | bytes 1310752 | tf_op jit(solution)/shard_map/ppermute | solution.py:15
  396.2 1.1 fusion.20
  397.2 1.8 fusion.11
  399.1 152.8 %all-reduce.3.cloned.1.call-done = (f32[5120,16]{0,1:T(8,128)}, f32[16,5120]{1,0:T(8,128)}) async-done(((f32[5120,16]{0,1:T(8,128)}, f32[16,5120]{1,0:T(8,128)}), (f32[5120,16]{0,1:T(8,128)}, f32[16,5120]{1,0:T(8,128)})) %all-reduce.3.cloned.1.call-update) | async-done | bytes 655376 | tf_op jit(solution)/shard_map/psum | solution.py:66
  551.9 1.7 multiply_bitcast_fusion
  553.7 1.7 multiply_bitcast_fusion.1
  555.4 2.5 copy.13
  (12 shorter events, 1.4 us)
Async XLA Ops:
  7.2 10.8 %copy-start = (bf16[1,16,5120]{2,1,0:T(8,128)(2,1)S(1)}, bf16[1,16,5120]{2,1,0:T(8,128)(2,1)}, u32[]{:S(2)}) copy-start(bf16[1,16,5120]{2,1,0:T(8,128)(2,1)} %param.10) | copy-start | bytes 491524
  7.2 9.4 %copy-start.1 = (bf16[1,128,5120]{2,1,0:T(8,128)(2,1)S(1)}, bf16[1,128,5120]{2,1,0:T(8,128)(2,1)}, u32[]{:S(2)}) copy-start(bf16[1,128,5120]{2,1,0:T(8,128)(2,1)} %param.6) | copy-start | bytes 3932164
  7.2 544.7 %all-reduce.3.cloned.1.call-start = ((), (), s32[]{:S(2)}) async-start(), calls=%async_computation | async-start | bytes 1310720 | tf_op jit(solution)/shard_map/psum | solution.py:66
  7.2 18.5 %collective-permute-start.5 = (bf16[128,5120]{1,0:T(8,128)(2,1)}, bf16[128,5120]{1,0:T(8,128)(2,1)}, u32[]{:S(2)}, u32[]{:S(2)}) collective-permute-start(bf16[128,5120]{1,0:T(8,128)(2,1)} %bitcast.42), channel_id=1, source_target_pairs={{0,448},{64,0},{128,64},{192,128},{256,192},{320,256},{384,320},{4... | collective-permute-start | bytes 3932168 | tf_op jit(solution)/shard_map/ppermute | solution.py:20
  18.5 32.2 %collective-permute-start = (bf16[128,5120]{1,0:T(8,128)(2,1)S(1)}, bf16[128,5120]{1,0:T(8,128)(2,1)}, u32[]{:S(2)}, u32[]{:S(2)}) collective-permute-start(bf16[128,5120]{1,0:T(8,128)(2,1)S(1)} %fusion), channel_id=1, source_target_pairs={{0,1},{1,0},{2,3},{3,2},{4,5},{5,4},{6,7},{7,6},{8,9},{9,8},{10,11... | collective-permute-start | bytes 3932168 | tf_op jit(solution)/shard_map/ppermute | solution.py:15
  25.8 73.7 %collective-permute-start.6 = (bf16[128,5120]{1,0:T(8,128)(2,1)}, bf16[128,5120]{1,0:T(8,128)(2,1)}, u32[]{:S(2)}, u32[]{:S(2)}) collective-permute-start(bf16[128,5120]{1,0:T(8,128)(2,1)} %collective-permute-done.5), channel_id=1, source_target_pairs={{0,1},{1,0},{2,3},{3,2},{4,5},{5,4},{6,7},{7,6},{8,9},{9,8},{10,11... | collective-permute-start | bytes 3932168 | tf_op jit(solution)/shard_map/ppermute | solution.py:15
  52.0 199.2 %collective-permute-start.1 = (bf16[128,5120]{1,0:T(8,128)(2,1)}, bf16[128,5120]{1,0:T(8,128)(2,1)}, u32[]{:S(2)}, u32[]{:S(2)}) collective-permute-start(bf16[128,5120]{1,0:T(8,128)(2,1)} %broadcast_select_fusion.1), channel_id=1, source_target_pairs={{0,2},{1,3},{2,0},{3,1},{4,6},{5,7},{6,4},{7,5},{8,10},{9,11},{10,... | collective-permute-start | bytes 3932168 | tf_op jit(solution)/shard_map/ppermute | solution.py:15
  101.9 177.3 %collective-permute-start.7 = (bf16[128,5120]{1,0:T(8,128)(2,1)}, bf16[128,5120]{1,0:T(8,128)(2,1)}, u32[]{:S(2)}, u32[]{:S(2)}) collective-permute-start(bf16[128,5120]{1,0:T(8,128)(2,1)} %broadcast_select_fusion), channel_id=1, source_target_pairs={{0,2},{1,3},{2,0},{3,1},{4,6},{5,7},{6,4},{7,5},{8,10},{9,11},{10,... | collective-permute-start | bytes 3932168 | tf_op jit(solution)/shard_map/ppermute | solution.py:15
  252.6 73.2 %collective-permute-start.2 = (bf16[128,5120]{1,0:T(8,128)(2,1)S(1)}, bf16[128,5120]{1,0:T(8,128)(2,1)}, u32[]{:S(2)}, u32[]{:S(2)}) collective-permute-start(bf16[128,5120]{1,0:T(8,128)(2,1)S(1)} %broadcast_select_fusion.3), channel_id=1, source_target_pairs={{0,4},{1,5},{2,6},{3,7},{4,0},{5,1},{6,2},{7,3},{8,12},{9,13},{10,... | collective-permute-start | bytes 3932168 | tf_op jit(solution)/shard_map/ppermute | solution.py:15
  281.8 85.0 %collective-permute-start.8 = (bf16[128,5120]{1,0:T(8,128)(2,1)}, bf16[128,5120]{1,0:T(8,128)(2,1)}, u32[]{:S(2)}, u32[]{:S(2)}) collective-permute-start(bf16[128,5120]{1,0:T(8,128)(2,1)} %broadcast_select_fusion.2), channel_id=1, source_target_pairs={{0,4},{1,5},{2,6},{3,7},{4,0},{5,1},{6,2},{7,3},{8,12},{9,13},{10,... | collective-permute-start | bytes 3932168 | tf_op jit(solution)/shard_map/ppermute | solution.py:15
  327.0 43.1 %collective-permute-start.3 = (bf16[128,5120]{1,0:T(8,128)(2,1)}, bf16[128,5120]{1,0:T(8,128)(2,1)}, u32[]{:S(2)}, u32[]{:S(2)}) collective-permute-start(bf16[128,5120]{1,0:T(8,128)(2,1)} %broadcast_select_fusion.5), channel_id=1, source_target_pairs={{0,8},{1,9},{2,10},{3,11},{4,12},{5,13},{6,14},{7,15},{8,0},{9,1},... | collective-permute-start | bytes 3932168 | tf_op jit(solution)/shard_map/ppermute | solution.py:15
  368.2 28.0 %collective-permute-start.9 = (bf16[128,5120]{1,0:T(8,128)(2,1)S(1)}, bf16[128,5120]{1,0:T(8,128)(2,1)}, u32[]{:S(2)}, u32[]{:S(2)}) collective-permute-start(bf16[128,5120]{1,0:T(8,128)(2,1)S(1)} %broadcast_select_fusion.4), channel_id=1, source_target_pairs={{0,8},{1,9},{2,10},{3,11},{4,12},{5,13},{6,14},{7,15},{8,0},{9,1},... | collective-permute-start | bytes 3932168 | tf_op jit(solution)/shard_map/ppermute | solution.py:15
  372.7 26.4 %collective-permute-start.4 = (bf16[128,5120]{1,0:T(8,128)(2,1)}, bf16[128,5120]{1,0:T(8,128)(2,1)}, u32[]{:S(2)}, u32[]{:S(2)}) collective-permute-start(bf16[128,5120]{1,0:T(8,128)(2,1)} %broadcast_select_fusion.7), channel_id=1, source_target_pairs={{0,64},{64,128},{128,192},{192,256},{256,320},{320,384},{384,448},... | collective-permute-start | bytes 3932168 | tf_op jit(solution)/shard_map/ppermute | solution.py:20
Sparse Core Ops, SparseCore 0:
  399.2 152.6 all-reduce.2
where the time goes:
time: 569 us; the launch traced here: 565 us
  waiting for transfers between devices  497 us (87%)
  starting transfers between devices  26.7 us (5%)
  other arithmetic  18.7 us (3%)
  between operations  14.8 us (3%)
    ppermute x8, waiting for transfers between devices, from_partner(): return lax.ppermute(value, axis, pairs)  339 us
    psum x1, waiting for transfers between devices, shards(): sum_down, sum_up = lax.psum((term_down, term_up), 'peer')  153 us
    ppermute x8, starting transfers between devices, from_partner(): return lax.ppermute(value, axis, pairs)  19.7 us
    select_n x7, other arithmetic, pick_moved(): return jnp.where(flag, moved, kept)  12.8 us
  transfers between devices with their start and end apart: 11, of which 9 were waited for; matrix products, arithmetic and copies ran while one was open for 4% of the time, Pallas kernels for 0%

commit v1 on v0

v1 whole, which is shorter than its diff:
```python
import functools

import jax
import jax.numpy as jnp
from jax import lax
from jax.experimental import pallas as pl
from jax.experimental.pallas import tpu as pltpu
from jax.sharding import PartitionSpec as P

MESH = pl.DeviceIdType.MESH
BF, F32 = jnp.bfloat16, jnp.float32
EPSILON = 1e-05
D, R, ROWS = 5120, 16, 128
SECTIONS, NY, NZ = 8, 8, 8
G = 16
C = 4
CH = ROWS // C
W = D // NY
TILES = W // 128


def wait_bytes(ref, sem):
    pltpu.make_async_copy(ref, ref, sem).wait()


def kernel(
    wiring, rows_hbm, ret_hbm, gain, down_t, up,
    fwd_hbm, gdown, gup,
    rows, ret, norm, out,
    s0, s1, s2, s3, p0, p1, p2, p3, q0, q1, q2, q3,
    up_prev, lat_send, lat_recv, lg_send, lg_recv,
    y_send, y_recv, z_send, z_recv, zg, fu, fd,
    send, recv, local, bulk_send, one_recv, two_recv,
):
    S, Pc, Q = (s0, s1, s2, s3), (p0, p1, p2, p3), (q0, q1, q2, q3)
    sec, peer = lax.axis_index("section"), lax.axis_index("peer")
    nxt, prv = lax.rem(sec + 1, SECTIONS), lax.rem(sec + SECTIONS - 1, SECTIONS)
    y, z = lax.div(peer, NZ), lax.rem(peer, NZ)
    g = lax.rem(peer, G)
    base = peer - g

    def member(k):
        z2 = lax.rem(z + lax.rem(k, NZ), NZ)
        b = lax.rem(lax.rem(y, 2) + lax.div(k, NZ), 2)
        return b * NZ + z2

    def y_peer(k):
        y2 = lax.rem(y + k, NY)
        return y2, y2 * NZ + z

    def z_peer(k):
        z2 = lax.rem(z + k, NZ)
        return z2, y * NZ + z2

    def put(src, dst, s_sem, r_sem, s, p):
        pltpu.make_async_remote_copy(
            src_ref=src, dst_ref=dst, send_sem=s_sem, recv_sem=r_sem, device_id=(s, p), device_id_type=MESH
        ).start()

    def loop(lo, hi, body):
        lax.fori_loop(lo, hi, lambda k, _: (body(k), None)[1], None)

    rows_in = [
        pltpu.make_async_copy(rows_hbm.at[pl.ds(CH * c, CH)], rows.at[pl.ds(CH * c, CH)], local.at[c]) for c in range(C)
    ]
    ret_in = pltpu.make_async_copy(ret_hbm, ret, local.at[C])
    for copy in rows_in:
        copy.start()
    ret_in.start()

    barrier = pltpu.get_barrier_semaphore()

    def greet(s, p):
        pl.semaphore_signal(barrier, inc=1, device_id=(s, p), device_id_type=MESH)

    loop(1, G, lambda k: greet(sec, base + member(k)))
    loop(0, G, lambda k: greet(nxt, base + member(k)))
    loop(0, G, lambda k: greet(prv, base + member(k)))
    loop(1, NY, lambda k: greet(sec, y_peer(k)[1]))
    loop(0, NY, lambda k: greet(prv, y_peer(k)[1]))
    loop(0, NY, lambda k: greet(nxt, y_peer(k)[1]))

    gain_f = gain[...].astype(F32)

    def normalise(i):
        part = pl.ds(pl.multiple_of(i * 16, 16), 16)
        x = rows[part, :].astype(F32)
        mean_square = jnp.mean(x * x, axis=-1, keepdims=True)
        norm[part, :] = (x * lax.rsqrt(mean_square + EPSILON) * gain_f).astype(BF)

    def latent_of(lo, n):
        return lax.dot_general(
            down_t[...], norm[pl.ds(lo, n), :], (((1,), (1,)), ((), ())), preferred_element_type=F32
        ).astype(BF)

    def outputs_of(c, latent):
        def columns(j):
            part = pl.ds(pl.multiple_of(j * W, W), W)
            o = rows[pl.ds(CH * c, CH), part].astype(F32) + lax.dot_general(
                latent, up[:, part], (((0,), (0,)), ((), ())), preferred_element_type=F32
            )
            o = o.astype(BF)
            S[c][j] = o[:16]
            S[c][j + NY] = o[16:]

        loop(0, NY, columns)
        Pc[c][g] = S[c][g]

    def first_hop(c):
        def one(k):
            j = member(k)
            put(S[c].at[j], Pc[c].at[g], bulk_send.at[c], one_recv.at[c], sec, base + j)

        loop(1, G, one)

    rows_in[0].wait()
    loop(0, CH // 16, normalise)
    latent_0 = latent_of(0, CH)
    outputs_of(0, latent_0)
    pl.semaphore_wait(barrier, 15 + 2 * G + 7 + 2 * NY)
    put(up, up_prev, send.at[0], recv.at[0], nxt, peer)
    first_hop(0)

    for c in range(1, C):
        rows_in[c].wait()
    loop(CH // 16, ROWS // 16, normalise)
    latent_r = latent_of(CH, ROWS - CH)
    latent = jnp.concatenate([latent_0, latent_r], axis=1)
    mask = jnp.bitwise_and(jnp.bitwise_xor(wiring[0, 0], peer), G - 1)
    pick = jnp.bitwise_xor(g, mask)

    def send_latent(k):
        r = member(k)
        hit = jnp.full((R, ROWS), pick, jnp.int32) == jnp.full((R, ROWS), r, jnp.int32)
        lat_send[r] = jnp.where(hit, latent.astype(F32), 0.0).astype(BF)
        put(lat_send.at[r], lat_recv.at[g], send.at[1], recv.at[1], nxt, base + r)

    loop(0, G, send_latent)
    outputs_of(1, latent[:, CH : 2 * CH])
    first_hop(1)

    ret_in.wait()
    wait_bytes(up_prev, recv.at[0])
    lg_send[...] = lax.dot_general(
        up_prev[...], ret[...], (((1,), (1,)), ((), ())), preferred_element_type=F32
    ).astype(BF)
    loop(0, G, lambda k: put(lg_send, lg_recv.at[g], send.at[2], recv.at[2], prv, base + member(k)))
    for c in range(2, C):
        outputs_of(c, latent[:, CH * c : CH * (c + 1)])
        first_hop(c)

    wait_bytes(lat_recv, recv.at[1])
    latent_here = lat_recv[0].astype(F32)
    for r in range(1, G):
        latent_here += lat_recv[r].astype(F32)
    latent_here = latent_here.astype(BF)
    wait_bytes(lg_recv, recv.at[2])
    grad_here = lg_recv[pick]

    def terms(j):
        part = pl.ds(pl.multiple_of(j * W, W), W)
        y_send[j, :R] = jnp.dot(latent_here, ret[:, part], preferred_element_type=F32).astype(BF)
        y_send[j, R:] = jnp.dot(grad_here, norm[:, part], preferred_element_type=F32).astype(BF)

    loop(0, NY, terms)
    y_recv[y] = y_send[y]

    def send_terms(k):
        y2, p = y_peer(k)
        put(y_send.at[y2], y_recv.at[y], send.at[3], recv.at[3], sec, p)

    loop(1, NY, send_terms)

    def second_hop(c):
        wait_bytes(Pc[c].at[pl.ds(0, G - 1)], one_recv.at[c])
        row = pl.ds(pl.multiple_of(CH * c + 16 * lax.div(g, NY), 16), 16)
        column = pl.ds(pl.multiple_of(lax.rem(g, NY) * W, W), W)

        def one(k):
            r = member(k)
            Q[c][r] = Pc[c][jnp.bitwise_xor(r, mask)]
            put(Q[c].at[r], out.at[row, column], bulk_send.at[C + c], two_recv.at[c], nxt, base + r)

        loop(0, G, one)

    second_hop(0)

    wait_bytes(y_recv.at[pl.ds(0, NY - 1)], recv.at[3])
    for i in range(2):
        part = pl.ds(R * i, R)
        total = y_recv[0, part].astype(F32)
        for k in range(1, NY):
            total += y_recv[k, part].astype(F32)
        for t in range(TILES):
            z_send[TILES * i + t] = total[:, 128 * t : 128 * (t + 1)].astype(BF)
    for t in range(2 * TILES, 2 * NZ):
        z_send[t] = jnp.zeros((R, 128), BF)
    z_recv[z] = z_send[pl.ds(2 * z, 2)]

    def send_sums(k):
        z2, p = z_peer(k)
        put(z_send.at[pl.ds(2 * z2, 2)], z_recv.at[z], send.at[4], recv.at[4], sec, p)

    loop(1, NZ, send_sums)
    second_hop(1)

    wait_bytes(z_recv.at[pl.ds(0, NZ - 1)], recv.at[4])
    total = z_recv[0].astype(F32)
    for k in range(1, NZ):
        total += z_recv[k].astype(F32)
    zg[pl.ds(2 * z, 2)] = total.astype(BF)

    def send_totals(k):
        _, p = z_peer(k)
        mine = zg.at[pl.ds(2 * z, 2)]
        put(mine, mine, send.at[5], recv.at[5], sec, p)

    loop(1, NZ, send_totals)
    second_hop(2)

    wait_bytes(zg.at[pl.ds(0, 2 * (NZ - 1))], recv.at[5])
    fd[y] = zg[TILES : 2 * TILES]

    def share_up(k):
        put(zg.at[pl.ds(0, TILES)], fu.at[y], send.at[6], recv.at[6], prv, y_peer(k)[1])

    def share_down(k):
        put(zg.at[pl.ds(TILES, TILES)], fd.at[y], send.at[7], recv.at[7], sec, y_peer(k)[1])

    loop(0, NY, share_up)
    loop(1, NY, share_down)
    second_hop(3)

    wait_bytes(fu, recv.at[6])
    wait_bytes(fd.at[pl.ds(0, NY - 1)], recv.at[7])
    scale = 1.0 / (NY * NZ)
    for k in range(NY):
        for t in range(TILES):
            part = pl.ds(W * k + 128 * t, 128)
            gup[:, part] = fu[k, t].astype(F32) * scale
            gdown[:, part] = fd[k, t].astype(F32) * scale

    rows_out = []
    for c in range(C):
        part = pl.ds(CH * c, CH)
        wait_bytes(out.at[part], two_recv.at[c])
        rows_out.append(pltpu.make_async_copy(out.at[part], fwd_hbm.at[part], local.at[C + 1 + c]))
        rows_out[c].start()
    for c in range(C):
        wait_bytes(S[c].at[pl.ds(0, G - 1)], bulk_send.at[c])
        wait_bytes(Q[c], bulk_send.at[C + c])
    wait_bytes(up_prev, send.at[0])
    wait_bytes(lat_send, send.at[1])
    wait_bytes(lg_recv, send.at[2])
    wait_bytes(y_send.at[pl.ds(0, NY - 1)], send.at[3])
    wait_bytes(z_send.at[pl.ds(0, 2 * (NZ - 1))], send.at[4])
    wait_bytes(zg.at[pl.ds(0, 2 * (NZ - 1))], send.at[5])
    wait_bytes(fu, send.at[6])
    wait_bytes(fd.at[pl.ds(0, NY - 1)], send.at[7])
    for copy in rows_out:
        copy.wait()


def shards(rows_in, returned, norm_gain, adapter_down, adapter_up, wiring):
    whole = pl.BlockSpec(memory_space=pltpu.VMEM)
    far = pl.BlockSpec(memory_space=pl.ANY)
    block = pltpu.VMEM((ROWS, D), BF)
    pieces = pltpu.VMEM((G, 16, W), BF)
    tiles = pltpu.VMEM((G, R, 128), BF)
    dma = pltpu.SemaphoreType.DMA
    fwd, down_t, up_sum = pl.pallas_call(
        kernel,
        out_shape=(
            jax.ShapeDtypeStruct((ROWS, D), BF),
            jax.ShapeDtypeStruct((R, D), F32),
            jax.ShapeDtypeStruct((R, D), F32),
        ),
        in_specs=[pl.BlockSpec(memory_space=pltpu.SMEM), far, far, whole, whole, whole],
        out_specs=(far, whole, whole),
        scratch_shapes=[block] * 4
        + [pieces] * (3 * C)
        + [pltpu.VMEM((R, D), BF), tiles, tiles, pltpu.VMEM((R, 128), BF), tiles]
        + [pltpu.VMEM((NY, 2 * R, W), BF)] * 2
        + [pltpu.VMEM((2 * NZ, R, 128), BF), pltpu.VMEM((NZ, 2, R, 128), BF), pltpu.VMEM((2 * NZ, R, 128), BF)]
        + [pltpu.VMEM((NY, TILES, R, 128), BF)] * 2
        + [dma((8,)), dma((8,)), dma((2 * C + 1,)), dma((2 * C,)), dma((C,)), dma((C,))],
        compiler_params=pltpu.CompilerParams(collective_id=0, has_side_effects=True, vmem_limit_bytes=40 << 20),
        name="adapter_step",
    )(wiring, rows_in[0], returned[0], norm_gain, adapter_down[0].T, adapter_up[0])
    return fwd[None], down_t.T[None], up_sum[None]


def solution(mesh):
    in_specs = (
        P("section", "peer", None),
        P("section", "peer", None),
        P("section", None),
        P("section", None, None),
        P("section", None, None),
        P("section", "peer"),
    )
    out_specs = (P("section", "peer", None), P("section", None, None), P("section", None, None))
    return jax.shard_map(shards, mesh=mesh, in_specs=in_specs, out_specs=out_specs, check_vma=False)
```

time: 569 us -> 98.5 us (0.17)
  the two profiles are of different devices: /device:TPU:1 before, /device:TPU:3 now
where the time goes in v1:
time: 98.5 us; the launch traced here: 98.2 us
  Pallas kernels  89.3 us (91%)
  local copies, waits for them, and re-layouts  7.69 us (8%)
  between operations  1.3 us (1%)
    pallas_call x1, Pallas kernels, shards(): pl.pallas_call(kernel, out_shape=(jax.ShapeDtypeStruct((ROWS, D), BF), ja...  89.3 us
    unnamed x13, local copies, waits for them, and re-layouts  7.69 us

profile of v1, /device:TPU:3, one launch (start us, length us, event | category | flops | bytes accessed | tf_op | source)
XLA Modules:
  0.0 98.2 jit_solution(16409159681585731355)
XLA Ops:
  1.3 0.0 copy-start
  1.3 1.3 %copy-done = bf16[1,128,5120]{2,1,0:T(8,128)(2,1)S(1)} copy-done((bf16[1,128,5120]{2,1,0:T(8,128)(2,1)S(1)}, bf16[1,128,5120]{2,1,0:T(8,128)(2,1)}, u32[]{:S(2)}) %copy-start) | copy-done | bytes 1310744
  2.6 0.0 copy-start.1
  2.6 1.3 %copy-done.1 = bf16[1,128,5120]{2,1,0:T(8,128)(2,1)S(1)} copy-done((bf16[1,128,5120]{2,1,0:T(8,128)(2,1)S(1)}, bf16[1,128,5120]{2,1,0:T(8,128)(2,1)}, u32[]{:S(2)}) %copy-start.1) | copy-done | bytes 1310744
  3.9 0.0 copy-start.2
  3.9 0.9 copy-done.2
  4.8 0.0 copy-start.3
  4.8 0.9 copy-done.3
  5.7 0.0 copy-start.4
  5.7 0.7 copy-done.4
  6.5 89.3 %adapter_step.1 = (bf16[128,5120]{1,0:T(8,128)(2,1)S(1)}, f32[16,5120]{1,0:T(8,128)S(1)}, f32[16,5120]{1,0:T(8,128)S(1)}) custom-call(s32[1,1]{1,0:T(1,128)S(6)} %copy.12.wiring, bf16[128,5120]{1,0:T(8,128)(2,1)S(1)} %bitcast.11, bf16[128,5120]{1,0:T(8,128)(2,1)S(1)} %bitcast.12, bf16[1,5120]{1,0:T(2,128)(2,1)S(1)} %copy-done.4, ...), custom_call_target="tpu_custom_call" | custom-call | tf_op jit(solution)/shard_map/adapter_step/pallas_call | solution.py:271
  95.7 1.1 %copy.13 = bf16[1,128,5120]{2,1,0:T(8,128)(2,1)} copy(bf16[1,128,5120]{2,1,0:T(8,128)(2,1)S(1)} %bitcast.13) | data formatting | bytes 2621440
  96.8 0.7 copy.14
  97.5 0.7 copy.15
Async XLA Ops:
  1.3 1.3 %copy-start = (bf16[1,128,5120]{2,1,0:T(8,128)(2,1)S(1)}, bf16[1,128,5120]{2,1,0:T(8,128)(2,1)}, u32[]{:S(2)}) copy-start(bf16[1,128,5120]{2,1,0:T(8,128)(2,1)} %param.6) | copy-start | bytes 3932164
  2.6 1.3 %copy-start.1 = (bf16[1,128,5120]{2,1,0:T(8,128)(2,1)S(1)}, bf16[1,128,5120]{2,1,0:T(8,128)(2,1)}, u32[]{:S(2)}) copy-start(bf16[1,128,5120]{2,1,0:T(8,128)(2,1)} %param.7) | copy-start | bytes 3932164
  3.9 0.9 copy-start.2
  4.8 0.9 copy-start.3
  5.7 0.7 copy-start.4

commit v2 on v1

v2 whole, which is shorter than its diff:
```python
import functools

import jax
import jax.numpy as jnp
from jax import lax
from jax.experimental import pallas as pl
from jax.experimental.pallas import tpu as pltpu
from jax.sharding import PartitionSpec as P

MESH = pl.DeviceIdType.MESH
BF, F32 = jnp.bfloat16, jnp.float32
EPSILON = 1e-05
D, R, ROWS = 5120, 16, 128
SECTIONS, NY, NZ = 8, 8, 8
G = 16
C = 4
CH = ROWS // C
W = D // NY
TILES = W // 128
OWNERS = TILES
WINDOW = 16
ORDER = "c0 N U L a0 c1 G a1 c2 T a2 c3 b0 Y a3 b1 Z b2 d3 F e3 E o0 o1 o2 o3"


def wait_bytes(ref, sem):
    pltpu.make_async_copy(ref, ref, sem).wait()


def kernel(
    wiring, rows_hbm, ret_hbm, gain_hbm, down_hbm, up_hbm,
    out, gdown, gup,
    rows, ret, norm, gain, down_t, up,
    s0, s1, s2, s3, p0, p1, p2, p3, q0, q1, q2, q3,
    up_prev, lat_send, lat_recv, lg_send, lg_recv,
    y_send, y_recv, z_send, z_recv, zg, fu, fd,
    send, recv, local, bulk_send, one_recv, two_recv,
):
    S, Pc, Q = (s0, s1, s2, s3), (p0, p1, p2, p3), (q0, q1, q2, q3)
    sec, peer = lax.axis_index("section"), lax.axis_index("peer")
    nxt, prv = lax.rem(sec + 1, SECTIONS), lax.rem(sec + SECTIONS - 1, SECTIONS)
    y, z = lax.div(peer, NZ), lax.rem(peer, NZ)
    g = lax.rem(peer, G)
    base = peer - g

    def member(k):
        z2 = lax.rem(z + lax.rem(k, NZ), NZ)
        b = lax.rem(lax.rem(y, 2) + lax.div(k, NZ), 2)
        return b * NZ + z2

    def y_peer(k):
        y2 = lax.rem(y + k, NY)
        return y2, y2 * NZ + z

    def z_peer(k):
        z2 = lax.rem(z + k, NZ)
        return z2, y * NZ + z2

    def put(src, dst, s_sem, r_sem, s, p):
        pltpu.make_async_remote_copy(
            src_ref=src, dst_ref=dst, send_sem=s_sem, recv_sem=r_sem, device_id=(s, p), device_id_type=MESH
        ).start()

    def loop(lo, hi, body):
        lax.fori_loop(lo, hi, lambda k, _: (body(k), None)[1], None)

    def load(src, dst, i):
        copy = pltpu.make_async_copy(src, dst, local.at[i])
        copy.start()
        return copy

    chunk = [pl.ds(CH * c, CH) for c in range(C)]
    rows_in = [load(rows_hbm.at[chunk[0]], rows.at[chunk[0]], 0)]
    gain_in, down_in = load(gain_hbm, gain, C + 1), load(down_hbm, down_t, C + 2)
    up_in = load(up_hbm, up, C + 3)
    rows_in += [load(rows_hbm.at[chunk[c]], rows.at[chunk[c]], c) for c in range(1, C)]
    ret_in = load(ret_hbm, ret, C)

    barrier = pltpu.get_barrier_semaphore()

    def greet(s, p):
        pl.semaphore_signal(barrier, inc=1, device_id=(s, p), device_id_type=MESH)

    loop(1, G, lambda k: greet(sec, base + member(k)))
    loop(0, G, lambda k: greet(nxt, base + member(k)))
    loop(0, G, lambda k: greet(prv, base + member(k)))
    loop(1, NY, lambda k: greet(sec, y_peer(k)[1]))
    loop(0, NY, lambda k: greet(prv, y_peer(k)[1]))
    loop(0, NY, lambda k: greet(nxt, y_peer(k)[1]))

    mask = jnp.bitwise_and(jnp.bitwise_xor(wiring[0, 0], peer), G - 1)
    pick = jnp.bitwise_xor(g, mask)
    latents, sent = {}, []

    def normalise(i):
        part = pl.ds(pl.multiple_of(i * 16, 16), 16)
        x = rows[part, :].astype(F32)
        mean_square = jnp.mean(x * x, axis=-1, keepdims=True)
        norm[part, :] = (x * lax.rsqrt(mean_square + EPSILON) * gain[...].astype(F32)).astype(BF)

    def latent_of(lo, n):
        loop(lo // 16, (lo + n) // 16, normalise)
        return lax.dot_general(
            down_t[...], norm[pl.ds(lo, n), :], (((1,), (1,)), ((), ())), preferred_element_type=F32
        ).astype(BF)

    def bulk(lo, hi, one):
        first = len(sent) - lo
        sent.extend(range(lo, hi))
        free = min(max(lo, WINDOW - first), hi)
        slot = lambda k: bulk_send.at[lax.rem(first + k, WINDOW)]

        def later(k):
            wait_bytes(S[0].at[0], slot(k))
            one(k, slot(k))

        loop(lo, free, lambda k: one(k, slot(k)))
        loop(free, hi, later)

    def outputs_of(c):
        latent = latents[c]

        def columns(j):
            part = pl.ds(pl.multiple_of(j * W, W), W)
            o = rows[chunk[c], part].astype(F32) + lax.dot_general(
                latent, up[:, part], (((0,), (0,)), ((), ())), preferred_element_type=F32
            )
            o = o.astype(BF)
            S[c][j] = o[:16]
            S[c][j + NY] = o[16:]

        loop(0, NY, columns)
        Pc[c][g] = S[c][g]

    def all_here():
        pl.semaphore_wait(barrier, 15 + 2 * G + 7 + 2 * NY)
        put(up, up_prev, send.at[0], recv.at[0], nxt, peer)

    def first_hop(c):
        def one(k, sem):
            j = member(k)
            put(S[c].at[j], Pc[c].at[g], sem, one_recv.at[c], sec, base + j)

        bulk(1, G, one)

    def second_hop(c, lo=0, hi=G):
        if lo == 0:
            wait_bytes(Pc[c].at[pl.ds(0, G - 1)], one_recv.at[c])
        row = pl.ds(pl.multiple_of(CH * c + 16 * lax.div(g, NY), 16), 16)
        column = pl.ds(pl.multiple_of(lax.rem(g, NY) * W, W), W)

        def one(k, sem):
            r = member(k)
            Q[c][r] = Pc[c][jnp.bitwise_xor(r, mask)]
            put(Q[c].at[r], out.at[row, column], sem, two_recv.at[c], nxt, base + r)

        bulk(lo, hi, one)

    def second_hop_near(c):
        second_hop(c, 0, G // 2)

    def second_hop_far(c):
        second_hop(c, G // 2, G)

    def other_latents():
        for c in range(1, C):
            rows_in[c].wait()
        rest = latent_of(CH, ROWS - CH)
        for c in range(1, C):
            latents[c] = rest[:, CH * (c - 1) : CH * c]
        latents["all"] = jnp.concatenate([latents[0], rest], axis=1).astype(F32)

    def send_latents():
        latent = latents["all"]

        def one(k):
            r = member(k)
            hit = jnp.full((R, ROWS), pick, jnp.int32) == jnp.full((R, ROWS), r, jnp.int32)
            lat_send[r] = jnp.where(hit, latent, 0.0).astype(BF)
            put(lat_send.at[r], lat_recv.at[g], send.at[1], recv.at[1], nxt, base + r)

        loop(0, G, one)

    def send_latent_grads():
        ret_in.wait()
        wait_bytes(up_prev, recv.at[0])
        lg_send[...] = lax.dot_general(
            up_prev[...], ret[...], (((1,), (1,)), ((), ())), preferred_element_type=F32
        ).astype(BF)
        loop(0, G, lambda k: put(lg_send, lg_recv.at[g], send.at[2], recv.at[2], prv, base + member(k)))

    def send_terms():
        wait_bytes(lat_recv, recv.at[1])
        latent_here = lat_recv[0].astype(F32)
        for r in range(1, G):
            latent_here += lat_recv[r].astype(F32)
        latent_here = latent_here.astype(BF)
        wait_bytes(lg_recv, recv.at[2])
        grad_here = lg_recv[pick]

        def terms(j):
            part = pl.ds(pl.multiple_of(j * W, W), W)
            y_send[j, :R] = jnp.dot(latent_here, ret[:, part], preferred_element_type=F32).astype(BF)
            y_send[j, R:] = jnp.dot(grad_here, norm[:, part], preferred_element_type=F32).astype(BF)

        loop(0, NY, terms)
        y_recv[y] = y_send[y]

        def one(k):
            y2, p = y_peer(k)
            put(y_send.at[y2], y_recv.at[y], send.at[3], recv.at[3], sec, p)

        loop(1, NY, one)

    def send_y_sums():
        wait_bytes(y_recv.at[pl.ds(0, NY - 1)], recv.at[3])
        for i in range(2):
            part = pl.ds(R * i, R)
            total = y_recv[0, part].astype(F32)
            for k in range(1, NY):
                total += y_recv[k, part].astype(F32)
            for t in range(TILES):
                z_send[TILES * i + t] = total[:, 128 * t : 128 * (t + 1)].astype(BF)

        @pl.when(z < OWNERS)
        def _():
            z_recv[z] = z_send[pl.ds(2 * z, 2)]

        def one(k):
            z2, p = z_peer(k)

            @pl.when(z2 < OWNERS)
            def _():
                put(z_send.at[pl.ds(2 * z2, 2)], z_recv.at[z], send.at[4], recv.at[4], sec, p)

        loop(1, NZ, one)

    def send_z_sums():
        @pl.when(z < OWNERS)
        def _():
            wait_bytes(z_recv.at[pl.ds(0, NZ - 1)], recv.at[4])
            total = z_recv[0].astype(F32)
            for k in range(1, NZ):
                total += z_recv[k].astype(F32)
            zg[pl.ds(2 * z, 2)] = total.astype(BF)

            def one(k):
                _, p = z_peer(k)
                mine = zg.at[pl.ds(2 * z, 2)]
                put(mine, mine, send.at[5], recv.at[5], sec, p)

            loop(1, NZ, one)

    def wait_owners(sem):
        @pl.when(z < OWNERS)
        def _():
            wait_bytes(zg.at[pl.ds(0, 2 * (OWNERS - 1))], sem)

        @pl.when(z >= OWNERS)
        def _():
            wait_bytes(zg.at[pl.ds(0, 2 * OWNERS)], sem)

    def send_totals():
        wait_owners(recv.at[5])
        fd[y] = zg[TILES : 2 * TILES]

        def share_up(k):
            put(zg.at[pl.ds(0, TILES)], fu.at[y], send.at[6], recv.at[6], prv, y_peer(k)[1])

        def share_down(k):
            put(zg.at[pl.ds(TILES, TILES)], fd.at[y], send.at[7], recv.at[7], sec, y_peer(k)[1])

        loop(0, NY, share_up)
        loop(1, NY, share_down)

    def gradients_out():
        wait_bytes(fu, recv.at[6])
        wait_bytes(fd.at[pl.ds(0, NY - 1)], recv.at[7])
        scale = 1.0 / (NY * NZ)
        for k in range(NY):
            for t in range(TILES):
                part = pl.ds(W * k + 128 * t, 128)
                gup[:, part] = fu[k, t].astype(F32) * scale
                gdown[:, part] = fd[k, t].astype(F32) * scale

    def rows_there(c):
        wait_bytes(out.at[chunk[c]], two_recv.at[c])

    rows_in[0].wait()
    gain_in.wait()
    down_in.wait()
    latents[0] = latent_of(0, CH)
    up_in.wait()
    steps = {
        "U": all_here, "N": other_latents, "L": send_latents, "G": send_latent_grads, "T": send_terms,
        "Y": send_y_sums, "Z": send_z_sums, "F": send_totals, "E": gradients_out,
    }
    for step in ORDER.split():
        if step in steps:
            steps[step]()
        else:
            {"c": outputs_of, "a": first_hop, "b": second_hop, "d": second_hop_near, "e": second_hop_far, "o": rows_there}[step[0]](int(step[1]))
    wait_bytes(up_prev, send.at[0])
    wait_bytes(lat_send, send.at[1])
    wait_bytes(lg_recv, send.at[2])
    wait_bytes(y_send.at[pl.ds(0, NY - 1)], send.at[3])
    wait_owners(send.at[4])

    @pl.when(z < OWNERS)
    def _():
        wait_bytes(zg.at[pl.ds(0, 2 * (NZ - 1))], send.at[5])

    wait_bytes(fu, send.at[6])
    wait_bytes(fd.at[pl.ds(0, NY - 1)], send.at[7])
    loop(0, WINDOW, lambda k: wait_bytes(S[0].at[0], bulk_send.at[k]))


def copy_out(*refs):
    sems = refs[-1]
    copies = [pltpu.make_async_copy(refs[i], refs[3 + i], sems.at[i]) for i in range(3)]
    for copy in copies:
        copy.start()
    for copy in copies:
        copy.wait()


def shards(rows_in, returned, norm_gain, adapter_down, adapter_up, wiring):
    whole = pl.BlockSpec(memory_space=pltpu.VMEM)
    far = pl.BlockSpec(memory_space=pltpu.HBM)
    anywhere = pl.BlockSpec(memory_space=pl.ANY)
    block = pltpu.VMEM((ROWS, D), BF)
    pieces = pltpu.VMEM((G, 16, W), BF)
    tiles = pltpu.VMEM((G, R, 128), BF)
    dma = pltpu.SemaphoreType.DMA
    operands = rows_in[0], returned[0], norm_gain, adapter_down[0].T, adapter_up[0]
    results = pl.pallas_call(
        kernel,
        out_shape=(
            jax.ShapeDtypeStruct((ROWS, D), BF),
            jax.ShapeDtypeStruct((R, D), F32),
            jax.ShapeDtypeStruct((R, D), F32),
        ),
        in_specs=[pl.BlockSpec(memory_space=pltpu.SMEM), far, far, far, far, far],
        out_specs=(anywhere, whole, whole),
        scratch_shapes=[block] * 3
        + [pltpu.VMEM((1, D), BF), pltpu.VMEM((R, D), BF), pltpu.VMEM((R, D), BF)]
        + [pieces] * (3 * C)
        + [pltpu.VMEM((R, D), BF), tiles, tiles, pltpu.VMEM((R, 128), BF), tiles]
        + [pltpu.VMEM((NY, 2 * R, W), BF)] * 2
        + [pltpu.VMEM((2 * NZ, R, 128), BF), pltpu.VMEM((NZ, 2, R, 128), BF), pltpu.VMEM((2 * NZ, R, 128), BF)]
        + [pltpu.VMEM((NY, TILES, R, 128), BF)] * 2
        + [dma((8,)), dma((8,)), dma((C + 4,)), dma((WINDOW,)), dma((C,)), dma((C,))],
        compiler_params=pltpu.CompilerParams(collective_id=0, has_side_effects=True, vmem_limit_bytes=40 << 20),
        name="adapter_step",
    )(wiring, *(pltpu.with_memory_space_constraint(v, pltpu.HBM) for v in operands))
    fwd, down_sum, up_sum = pl.pallas_call(
        copy_out,
        out_shape=tuple(jax.ShapeDtypeStruct(v.shape, v.dtype) for v in results),
        in_specs=[anywhere] * 3,
        out_specs=(anywhere,) * 3,
        scratch_shapes=[dma((3,))],
        name="copy_out",
    )(*(pltpu.with_memory_space_constraint(v, pltpu.VMEM) for v in results))
    return fwd[None], down_sum.T[None], up_sum[None]


def solution(mesh):
    in_specs = (
        P("section", "peer", None),
        P("section", "peer", None),
        P("section", None),
        P("section", None, None),
        P("section", None, None),
        P("section", "peer"),
    )
    out_specs = (P("section", "peer", None), P("section", None, None), P("section", None, None))
    return jax.shard_map(shards, mesh=mesh, in_specs=in_specs, out_specs=out_specs, check_vma=False)
```

time: 98.5 us -> 91.2 us (0.926)
  the two profiles are of different devices: /device:TPU:3 before, /device:TPU:1 now
where the time goes in v2:
time: 91.2 us; the launch traced here: 89.9 us
  Pallas kernels  88.6 us (97%)
  between operations  1.29 us (1%)
    pallas_call x1, Pallas kernels, shards(): pl.pallas_call(kernel, out_shape=(jax.ShapeDtypeStruct((ROWS, D), BF), ja...  87.3 us

profile of v2, /device:TPU:1, one launch (start us, length us, event | category | flops | bytes accessed | tf_op | source)
XLA Modules:
  0.0 89.9 jit_solution(16031973657252145652)
XLA Ops:
  1.3 87.3 %adapter_step.1 = (bf16[128,5120]{1,0:T(8,128)(2,1)S(1)}, f32[16,5120]{1,0:T(8,128)S(1)}, f32[16,5120]{1,0:T(8,128)S(1)}) custom-call(s32[1,1]{1,0:T(1,128)S(6)} %copy.9.wiring, bf16[128,5120]{1,0:T(8,128)(2,1)} %bitcast.11, bf16[128,5120]{1,0:T(8,128)(2,1)} %bitcast.12, bf16[1,5120]{1,0:T(2,128)(2,1)} %gain_hbm.1, bf16[16,5120]{1,0:T(8,128)(2,1)} %bitcast.13, ...), custom_call_target="tpu_custom_call" | custom-call | tf_op jit(solution)/shard_map/adapter_step/pallas_call | solution.py:335
  88.6 1.3 %copy_out.1 = (bf16[128,5120]{1,0:T(8,128)(2,1)}, f32[16,5120]{1,0:T(8,128)}, f32[16,5120]{1,0:T(8,128)}) custom-call(bf16[128,5120]{1,0:T(8,128)(2,1)S(1)} %get-tuple-element.9.refs_0_, f32[16,5120]{1,0:T(8,128)S(1)} %get-tuple-element.10.refs_1_, f32[16,5120]{1,0:T(8,128)S(1)} %get-tuple-element.11.refs_2_), custom_call_target="tpu_custom_call" | custom-call | tf_op jit(solution)/shard_map/copy_out/pallas_call | solution.py:355

commit v3 on v2

--- a/solution.py
+++ b/solution.py
@@ -19,7 +19,11 @@
 TILES = W // 128
 OWNERS = TILES
 WINDOW = 16
-ORDER = "c0 N U L a0 c1 G a1 c2 T a2 c3 b0 Y a3 b1 Z b2 d3 F e3 E o0 o1 o2 o3"
+ORDER = (
+    "c0", "N", "U", "X", "a0", "L", "c1", "G", "a1", "c2",
+    "K", "c3", "a2", "T", "b0", "Y", "a3", "b1", "Z", "b2",
+    "d3", "F", "e3", "E", "o0", "o1", "o2", "o3",
+)
 
 
 def wait_bytes(ref, sem):
@@ -31,7 +35,7 @@
     out, gdown, gup,
     rows, ret, norm, gain, down_t, up,
     s0, s1, s2, s3, p0, p1, p2, p3, q0, q1, q2, q3,
-    up_prev, lat_send, lat_recv, lg_send, lg_recv,
+    up_prev, lat_send, lat_recv, lg_send, lg_recv, lat_here, lat_there, lg_here, lg_there,
     y_send, y_recv, z_send, z_recv, zg, fu, fd,
     send, recv, local, bulk_send, one_recv, two_recv,
 ):
@@ -43,7 +47,7 @@
     base = peer - g
 
     def member(k):
-        z2 = lax.rem(z + lax.rem(k, NZ), NZ)
+        z2 = lax.rem(z + 3 * lax.rem(k, NZ), NZ)
         b = lax.rem(lax.rem(y, 2) + lax.div(k, NZ), 2)
         return b * NZ + z2
 
@@ -87,9 +91,8 @@
     loop(0, NY, lambda k: greet(prv, y_peer(k)[1]))
     loop(0, NY, lambda k: greet(nxt, y_peer(k)[1]))
 
-    mask = jnp.bitwise_and(jnp.bitwise_xor(wiring[0, 0], peer), G - 1)
-    pick = jnp.bitwise_xor(g, mask)
     latents, sent = {}, []
+    pair = peer + NZ * (1 - 2 * lax.rem(y, 2))
 
     def normalise(i):
         part = pl.ds(pl.multiple_of(i * 16, 16), 16)
@@ -120,7 +123,7 @@
         latent = latents[c]
 
         def columns(j):
-            part = pl.ds(pl.multiple_of(j * W, W), W)
+            part = pl.ds(j * W, W)
             o = rows[chunk[c], part].astype(F32) + lax.dot_general(
                 latent, up[:, part], (((0,), (0,)), ((), ())), preferred_element_type=F32
             )
@@ -128,7 +131,8 @@
             S[c][j] = o[:16]
             S[c][j + NY] = o[16:]
 
-        loop(0, NY, columns)
+        for j in range(NY):
+            columns(j)
         Pc[c][g] = S[c][g]
 
     def all_here():
@@ -169,16 +173,25 @@
             latents[c] = rest[:, CH * (c - 1) : CH * c]
         latents["all"] = jnp.concatenate([latents[0], rest], axis=1).astype(F32)
 
+    def of_pair(there, here):
+        crossed = jnp.full((R, ROWS), mask_y, jnp.int32) == 1
+        return jnp.where(crossed, there[...].astype(F32), here[...].astype(F32))
+
+    def swap_latents():
+        lat_here[...] = latents["all"].astype(BF)
+        put(lat_here, lat_there, send.at[8], recv.at[8], sec, pair)
+
     def send_latents():
-        latent = latents["all"]
+        wait_bytes(lat_there, recv.at[8])
+        latent = of_pair(lat_there, lat_here)
 
         def one(k):
-            r = member(k)
-            hit = jnp.full((R, ROWS), pick, jnp.int32) == jnp.full((R, ROWS), r, jnp.int32)
-            lat_send[r] = jnp.where(hit, latent, 0.0).astype(BF)
-            put(lat_send.at[r], lat_recv.at[g], send.at[1], recv.at[1], nxt, base + r)
-
-        loop(0, G, one)
+            z2, p = z_peer(3 * k)
+            hit = jnp.full((R, ROWS), pick, jnp.int32) == jnp.full((R, ROWS), z2, jnp.int32)
+            lat_send[z2] = jnp.where(hit, latent, 0.0).astype(BF)
+            put(lat_send.at[z2], lat_recv.at[z], send.at[1], recv.at[1], nxt, p)
+
+        loop(0, NZ, one)
 
     def send_latent_grads():
         ret_in.wait()
@@ -186,16 +199,21 @@
         lg_send[...] = lax.dot_general(
             up_prev[...], ret[...], (((1,), (1,)), ((), ())), preferred_element_type=F32
         ).astype(BF)
-        loop(0, G, lambda k: put(lg_send, lg_recv.at[g], send.at[2], recv.at[2], prv, base + member(k)))
+        loop(0, NZ, lambda k: put(lg_send, lg_recv.at[z], send.at[2], recv.at[2], prv, z_peer(3 * k)[1]))
+
+    def swap_latent_grads():
+        wait_bytes(lg_recv, recv.at[2])
+        lg_here[...] = lg_recv[pick]
+        put(lg_here, lg_there, send.at[9], recv.at[9], sec, pair)
 
     def send_terms():
         wait_bytes(lat_recv, recv.at[1])
         latent_here = lat_recv[0].astype(F32)
-        for r in range(1, G):
+        for r in range(1, NZ):
             latent_here += lat_recv[r].astype(F32)
         latent_here = latent_here.astype(BF)
-        wait_bytes(lg_recv, recv.at[2])
-        grad_here = lg_recv[pick]
+        wait_bytes(lg_there, recv.at[9])
+        grad_here = of_pair(lg_there, lg_here).astype(BF)
 
         def terms(j):
             part = pl.ds(pl.multiple_of(j * W, W), W)
@@ -290,11 +308,14 @@
     down_in.wait()
     latents[0] = latent_of(0, CH)
     up_in.wait()
+    mask = jnp.bitwise_and(jnp.bitwise_xor(wiring[0, 0], peer), G - 1)
+    mask_z, mask_y = lax.rem(mask, NZ), lax.div(mask, NZ)
+    pick = jnp.bitwise_xor(z, mask_z)
     steps = {
-        "U": all_here, "N": other_latents, "L": send_latents, "G": send_latent_grads, "T": send_terms,
+        "U": all_here, "N": other_latents, "X": swap_latents, "L": send_latents, "K": swap_latent_grads, "G": send_latent_grads, "T": send_terms,
         "Y": send_y_sums, "Z": send_z_sums, "F": send_totals, "E": gradients_out,
     }
-    for step in ORDER.split():
+    for step in ORDER:
         if step in steps:
             steps[step]()
         else:
@@ -302,6 +323,8 @@
     wait_bytes(up_prev, send.at[0])
     wait_bytes(lat_send, send.at[1])
     wait_bytes(lg_recv, send.at[2])
+    wait_bytes(lat_there, send.at[8])
+    wait_bytes(lg_there, send.at[9])
     wait_bytes(y_send.at[pl.ds(0, NY - 1)], send.at[3])
     wait_owners(send.at[4])
 
@@ -329,7 +352,7 @@
     anywhere = pl.BlockSpec(memory_space=pl.ANY)
     block = pltpu.VMEM((ROWS, D), BF)
     pieces = pltpu.VMEM((G, 16, W), BF)
-    tiles = pltpu.VMEM((G, R, 128), BF)
+    tiles, tile = pltpu.VMEM((NZ, R, 128), BF), pltpu.VMEM((R, 128), BF)
     dma = pltpu.SemaphoreType.DMA
     operands = rows_in[0], returned[0], norm_gain, adapter_down[0].T, adapter_up[0]
     results = pl.pallas_call(
@@ -339,16 +362,17 @@
             jax.ShapeDtypeStruct((R, D), F32),
             jax.ShapeDtypeStruct((R, D), F32),
         ),
-        in_specs=[pl.BlockSpec(memory_space=pltpu.SMEM), far, far, far, far, far],
+        in_specs=[pl.BlockSpec(memory_space=pltpu.SMEM)] + [far] * 5,
         out_specs=(anywhere, whole, whole),
         scratch_shapes=[block] * 3
         + [pltpu.VMEM((1, D), BF), pltpu.VMEM((R, D), BF), pltpu.VMEM((R, D), BF)]
         + [pieces] * (3 * C)
-        + [pltpu.VMEM((R, D), BF), tiles, tiles, pltpu.VMEM((R, 128), BF), tiles]
+        + [pltpu.VMEM((R, D), BF), tiles, tiles, tile, tiles]
+        + [tile] * 4
         + [pltpu.VMEM((NY, 2 * R, W), BF)] * 2
         + [pltpu.VMEM((2 * NZ, R, 128), BF), pltpu.VMEM((NZ, 2, R, 128), BF), pltpu.VMEM((2 * NZ, R, 128), BF)]
         + [pltpu.VMEM((NY, TILES, R, 128), BF)] * 2
-        + [dma((8,)), dma((8,)), dma((C + 4,)), dma((WINDOW,)), dma((C,)), dma((C,))],
+        + [dma((10,)), dma((10,)), dma((C + 4,)), dma((WINDOW,)), dma((C,)), dma((C,))],
         compiler_params=pltpu.CompilerParams(collective_id=0, has_side_effects=True, vmem_limit_bytes=40 << 20),
         name="adapter_step",
     )(wiring, *(pltpu.with_memory_space_constraint(v, pltpu.HBM) for v in operands))

time: 91.2 us -> 88.8 us (0.974)
  Pallas kernels: 88.6 us -> 86.5 us
    pallas_call x1, Pallas kernels: 87.3 us -> 85.2 us  [shards(): pl.pallas_call(kernel, out_shape=(jax.ShapeDtypeStruct((ROWS, D), BF), ja...]
where the time goes in v3:
time: 88.8 us; the launch traced here: 87.8 us
  Pallas kernels  86.5 us (97%)
  between operations  1.29 us (1%)
    pallas_call x1, Pallas kernels, shards(): pl.pallas_call(kernel, out_shape=(jax.ShapeDtypeStruct((ROWS, D), BF), ja...  85.2 us

profile of v3, /device:TPU:1, one launch (start us, length us, event | category | flops | bytes accessed | tf_op | source)
XLA Modules:
  0.0 87.8 jit_solution(7173186049754739295)
XLA Ops:
  1.3 85.2 %adapter_step.1 = (bf16[128,5120]{1,0:T(8,128)(2,1)S(1)}, f32[16,5120]{1,0:T(8,128)S(1)}, f32[16,5120]{1,0:T(8,128)S(1)}) custom-call(s32[1,1]{1,0:T(1,128)S(6)} %copy.9.wiring, bf16[128,5120]{1,0:T(8,128)(2,1)} %bitcast.11, bf16[128,5120]{1,0:T(8,128)(2,1)} %bitcast.12, bf16[1,5120]{1,0:T(2,128)(2,1)} %gain_hbm.1, bf16[16,5120]{1,0:T(8,128)(2,1)} %bitcast.13, ...), custom_call_target="tpu_custom_call" | custom-call | tf_op jit(solution)/shard_map/adapter_step/pallas_call | solution.py:358
  86.5 1.3 %copy_out.1 = (bf16[128,5120]{1,0:T(8,128)(2,1)}, f32[16,5120]{1,0:T(8,128)}, f32[16,5120]{1,0:T(8,128)}) custom-call(bf16[128,5120]{1,0:T(8,128)(2,1)S(1)} %get-tuple-element.9.refs_0_, f32[16,5120]{1,0:T(8,128)S(1)} %get-tuple-element.10.refs_1_, f32[16,5120]{1,0:T(8,128)S(1)} %get-tuple-element.11.refs_2_), custom_call_target="tpu_custom_call" | custom-call | tf_op jit(solution)/shard_map/copy_out/pallas_call | solution.py:379

commit v4 on v3

--- a/solution.py
+++ b/solution.py
@@ -18,11 +18,11 @@
 W = D // NY
 TILES = W // 128
 OWNERS = TILES
-WINDOW = 16
+WINDOW = 22
 ORDER = (
     "c0", "N", "U", "X", "a0", "L", "c1", "G", "a1", "c2",
-    "K", "c3", "a2", "T", "b0", "Y", "a3", "b1", "Z", "b2",
-    "d3", "F", "e3", "E", "o0", "o1", "o2", "o3",
+    "K", "c3", "a2", "T", "b0", "Y", "a3", "d1", "Z", "e1",
+    "b2", "F", "b3", "E", "o0", "o1", "o2", "o3",
 )
 
 
@@ -45,6 +45,7 @@
     y, z = lax.div(peer, NZ), lax.rem(peer, NZ)
     g = lax.rem(peer, G)
     base = peer - g
+    own = lax.rem(3 * z, NZ)
 
     def member(k):
         z2 = lax.rem(z + 3 * lax.rem(k, NZ), NZ)
@@ -239,41 +240,42 @@
             for t in range(TILES):
                 z_send[TILES * i + t] = total[:, 128 * t : 128 * (t + 1)].astype(BF)
 
-        @pl.when(z < OWNERS)
+        @pl.when(own < OWNERS)
         def _():
-            z_recv[z] = z_send[pl.ds(2 * z, 2)]
+            z_recv[z] = z_send[pl.ds(2 * own, 2)]
 
         def one(k):
             z2, p = z_peer(k)
-
-            @pl.when(z2 < OWNERS)
+            theirs = lax.rem(3 * z2, NZ)
+
+            @pl.when(theirs < OWNERS)
             def _():
-                put(z_send.at[pl.ds(2 * z2, 2)], z_recv.at[z], send.at[4], recv.at[4], sec, p)
+                put(z_send.at[pl.ds(2 * theirs, 2)], z_recv.at[z], send.at[4], recv.at[4], sec, p)
 
         loop(1, NZ, one)
 
     def send_z_sums():
-        @pl.when(z < OWNERS)
+        @pl.when(own < OWNERS)
         def _():
             wait_bytes(z_recv.at[pl.ds(0, NZ - 1)], recv.at[4])
             total = z_recv[0].astype(F32)
             for k in range(1, NZ):
                 total += z_recv[k].astype(F32)
-            zg[pl.ds(2 * z, 2)] = total.astype(BF)
+            zg[pl.ds(2 * own, 2)] = total.astype(BF)
 
             def one(k):
                 _, p = z_peer(k)
-                mine = zg.at[pl.ds(2 * z, 2)]
+                mine = zg.at[pl.ds(2 * own, 2)]
                 put(mine, mine, send.at[5], recv.at[5], sec, p)
 
             loop(1, NZ, one)
 
     def wait_owners(sem):
-        @pl.when(z < OWNERS)
+        @pl.when(own < OWNERS)
         def _():
             wait_bytes(zg.at[pl.ds(0, 2 * (OWNERS - 1))], sem)
 
-        @pl.when(z >= OWNERS)
+        @pl.when(own >= OWNERS)
         def _():
             wait_bytes(zg.at[pl.ds(0, 2 * OWNERS)], sem)
 
@@ -328,7 +330,7 @@
     wait_bytes(y_send.at[pl.ds(0, NY - 1)], send.at[3])
     wait_owners(send.at[4])
 
-    @pl.when(z < OWNERS)
+    @pl.when(own < OWNERS)
     def _():
         wait_bytes(zg.at[pl.ds(0, 2 * (NZ - 1))], send.at[5])
 

time: 88.8 us -> 88.6 us (level)
  no operation moved by 1% of the time
where the time goes in v4:
time: 88.6 us; the launch traced here: 88.4 us
  Pallas kernels  87.1 us (98%)
  between operations  1.29 us (1%)
    pallas_call x1, Pallas kernels, shards(): pl.pallas_call(kernel, out_shape=(jax.ShapeDtypeStruct((ROWS, D), BF), ja...  85.9 us

profile of v4, /device:TPU:1, one launch (start us, length us, event | category | flops | bytes accessed | tf_op | source)
XLA Modules:
  0.0 88.4 jit_solution(14704869187476354241)
XLA Ops:
  1.3 85.9 %adapter_step.1 = (bf16[128,5120]{1,0:T(8,128)(2,1)S(1)}, f32[16,5120]{1,0:T(8,128)S(1)}, f32[16,5120]{1,0:T(8,128)S(1)}) custom-call(s32[1,1]{1,0:T(1,128)S(6)} %copy.9.wiring, bf16[128,5120]{1,0:T(8,128)(2,1)} %bitcast.11, bf16[128,5120]{1,0:T(8,128)(2,1)} %bitcast.12, bf16[1,5120]{1,0:T(2,128)(2,1)} %gain_hbm.1, bf16[16,5120]{1,0:T(8,128)(2,1)} %bitcast.13, ...), custom_call_target="tpu_custom_call" | custom-call | tf_op jit(solution)/shard_map/adapter_step/pallas_call | solution.py:360
  87.1 1.3 %copy_out.1 = (bf16[128,5120]{1,0:T(8,128)(2,1)}, f32[16,5120]{1,0:T(8,128)}, f32[16,5120]{1,0:T(8,128)}) custom-call(bf16[128,5120]{1,0:T(8,128)(2,1)S(1)} %get-tuple-element.9.refs_0_, f32[16,5120]{1,0:T(8,128)S(1)} %get-tuple-element.10.refs_1_, f32[16,5120]{1,0:T(8,128)S(1)} %get-tuple-element.11.refs_2_), custom_call_target="tpu_custom_call" | custom-call | tf_op jit(solution)/shard_map/copy_out/pallas_call | solution.py:381

commit v5 on v3

--- a/solution.py
+++ b/solution.py
@@ -21,8 +21,8 @@
 WINDOW = 16
 ORDER = (
     "c0", "N", "U", "X", "a0", "L", "c1", "G", "a1", "c2",
-    "K", "c3", "a2", "T", "b0", "Y", "a3", "b1", "Z", "b2",
-    "d3", "F", "e3", "E", "o0", "o1", "o2", "o3",
+    "K", "c3", "a2", "T", "b0", "Y", "a3", "d1", "Z", "e1",
+    "b2", "F", "b3", "E", "o0", "o1", "o2", "o3",
 )
 
 

time: 88.8 us -> 88.2 us (level)
  the two profiles are of different devices: /device:TPU:1 before, /device:TPU:64 now
where the time goes in v5:
time: 88.2 us; the launch traced here: 88.1 us
  Pallas kernels  86.8 us (98%)
  between operations  1.29 us (1%)
    pallas_call x1, Pallas kernels, shards(): pl.pallas_call(kernel, out_shape=(jax.ShapeDtypeStruct((ROWS, D), BF), ja...  85.5 us

profile of v5, /device:TPU:64, one launch (start us, length us, event | category | flops | bytes accessed | tf_op | source)
XLA Modules:
  0.0 88.1 jit_solution(7156655382801207186)
XLA Ops:
  1.3 85.5 %adapter_step.1 = (bf16[128,5120]{1,0:T(8,128)(2,1)S(1)}, f32[16,5120]{1,0:T(8,128)S(1)}, f32[16,5120]{1,0:T(8,128)S(1)}) custom-call(s32[1,1]{1,0:T(1,128)S(6)} %copy.9.wiring, bf16[128,5120]{1,0:T(8,128)(2,1)} %bitcast.11, bf16[128,5120]{1,0:T(8,128)(2,1)} %bitcast.12, bf16[1,5120]{1,0:T(2,128)(2,1)} %gain_hbm.1, bf16[16,5120]{1,0:T(8,128)(2,1)} %bitcast.13, ...), custom_call_target="tpu_custom_call" | custom-call | tf_op jit(solution)/shard_map/adapter_step/pallas_call | solution.py:358
  86.8 1.3 %copy_out.1 = (bf16[128,5120]{1,0:T(8,128)(2,1)}, f32[16,5120]{1,0:T(8,128)}, f32[16,5120]{1,0:T(8,128)}) custom-call(bf16[128,5120]{1,0:T(8,128)(2,1)S(1)} %get-tuple-element.9.refs_0_, f32[16,5120]{1,0:T(8,128)S(1)} %get-tuple-element.10.refs_1_, f32[16,5120]{1,0:T(8,128)S(1)} %get-tuple-element.11.refs_2_), custom_call_target="tpu_custom_call" | custom-call | tf_op jit(solution)/shard_map/copy_out/pallas_call | solution.py:379

commit v6 on v5

--- a/solution.py
+++ b/solution.py
@@ -18,7 +18,7 @@
 W = D // NY
 TILES = W // 128
 OWNERS = TILES
-WINDOW = 16
+WINDOW = 22
 ORDER = (
     "c0", "N", "U", "X", "a0", "L", "c1", "G", "a1", "c2",
     "K", "c3", "a2", "T", "b0", "Y", "a3", "d1", "Z", "e1",

time: 88.2 us -> 88.7 us (level)
  the two profiles are of different devices: /device:TPU:64 before, /device:TPU:1 now
where the time goes in v6:
time: 88.7 us; the launch traced here: 88.6 us
  Pallas kernels  87.3 us (98%)
  between operations  1.29 us (1%)
    pallas_call x1, Pallas kernels, shards(): pl.pallas_call(kernel, out_shape=(jax.ShapeDtypeStruct((ROWS, D), BF), ja...  86 us

profile of v6, /device:TPU:1, one launch (start us, length us, event | category | flops | bytes accessed | tf_op | source)
XLA Modules:
  0.0 88.6 jit_solution(9823654249231740997)
XLA Ops:
  1.3 86.0 %adapter_step.1 = (bf16[128,5120]{1,0:T(8,128)(2,1)S(1)}, f32[16,5120]{1,0:T(8,128)S(1)}, f32[16,5120]{1,0:T(8,128)S(1)}) custom-call(s32[1,1]{1,0:T(1,128)S(6)} %copy.9.wiring, bf16[128,5120]{1,0:T(8,128)(2,1)} %bitcast.11, bf16[128,5120]{1,0:T(8,128)(2,1)} %bitcast.12, bf16[1,5120]{1,0:T(2,128)(2,1)} %gain_hbm.1, bf16[16,5120]{1,0:T(8,128)(2,1)} %bitcast.13, ...), custom_call_target="tpu_custom_call" | custom-call | tf_op jit(solution)/shard_map/adapter_step/pallas_call | solution.py:358
  87.3 1.3 %copy_out.1 = (bf16[128,5120]{1,0:T(8,128)(2,1)}, f32[16,5120]{1,0:T(8,128)}, f32[16,5120]{1,0:T(8,128)}) custom-call(bf16[128,5120]{1,0:T(8,128)(2,1)S(1)} %get-tuple-element.9.refs_0_, f32[16,5120]{1,0:T(8,128)S(1)} %get-tuple-element.10.refs_1_, f32[16,5120]{1,0:T(8,128)S(1)} %get-tuple-element.11.refs_2_), custom_call_target="tpu_custom_call" | custom-call | tf_op jit(solution)/shard_map/copy_out/pallas_call | solution.py:379
